TPU v7x, 32 devices: a whole 2x2x4 slice. The times are simulated.
32 devices in a mesh: runs: 2 (over x), gx: 16 (over z, y, core).
Axes of the slice: x: 2, y: 2, z: 4, core: 2. Of those that a mesh axis runs over, the one named last changes fastest.
Arguments:
- frac: float32 [3, 524288], P(None, ('runs', 'gx')), parts along dimension 1, may hold values from 0 to 1
- velocity: float32 [3, 524288], P(None, ('runs', 'gx')), parts along dimension 1, may hold values from -6 to 6
- mass: float32 [524288], P(('runs', 'gx')), parts along dimension 0, may hold values from 0.5 to 2
- particle_cell: int32 [524288], P(('runs', 'gx')), parts along dimension 0, may hold values from 0 to 8191, as said below
- tile_count: int32 [32], P(('runs', 'gx')), parts along dimension 0, may hold values from 2048 to 16384, as said below
- time_step: float32 [2], P('runs'), parts along dimension 0, may hold values from 0.1 to 0.2
Outputs:
- new_frac: float32 [3, 524288], P(None, ('runs', 'gx')), parts along dimension 1
- new_velocity: float32 [3, 524288], P(None, ('runs', 'gx')), parts along dimension 1
- next_step: float32 [2], P('runs'), parts along dimension 0
There are 2 independent parts, one for each index of `runs`. A program takes and returns all parts, laid end to end along the dimension named above; each array names one. Nothing has to cross between parts.
Inputs may be any that keep to these rules, and one draw needn't show every extreme that they name: `particle_cell`: within each tile the slots' cell numbers never fall; live slots come first and lie in cells with z <= 126; empty slots name the tile's last cell. `tile_count`: some tile is full in every run.
All inputs are finite; a program needn't handle non-finite values.
Results may differ from a plain program's by a relative error of at most 0.0003.
Values sent between devices are 32-bit elements; how exact they have to be, the bound alone decides.
No kernel may reach another device: no remote copies, remote signals or barrier semaphores. Data moves between devices by JAX's collectives and lax.ppermute only.
A program may use at most 64 MiB of HBM per device.

v0:
```python
import functools

import jax
import jax.numpy as jnp
from jax import lax
from jax.experimental import pallas as pl
from jax.experimental.pallas import tpu as pltpu
from jax.sharding import PartitionSpec as P

CX = 2
NY = 32
NZ = 128
ROWS = CX * NY
PAIRS = ROWS // 2
LAST = ROWS * NZ - 1
WIDE = 2 * NZ
BLOCK = 256
LANES = 128
GIVEN = 32
TAKEN = 32
SPREAD = 32
TABLE = 16

mass_floor = 0.25
stiffness = 2.0
press_floor = 1.0
grain_size = 0.5
inertia_ref = 0.3
mu_static = 0.38
mu_limit = 0.64
rate_floor = 0.5
gravity = (0.5, 0.0, -0.866)
flip_share = 0.95
courant = 0.4
wave_speed = 2.0
components = ((0, 3, 4), (3, 1, 5), (4, 5, 2))
f32 = jnp.float32
bf16 = jnp.bfloat16


def split_pair(values):
    high = values.astype(bf16)
    low = (values - high.astype(f32)).astype(bf16)
    return high, low


def relative(cells_ref, block, offset):
    return cells_ref[pl.ds(block * 2, 2), :] - offset


def one_hot(rel, wide):
    tall = (16, LANES)
    nodes = lax.broadcasted_iota(jnp.int32, tall, 0).astype(f32)
    one, zero = jnp.ones(tall, bf16), jnp.zeros(tall, bf16)
    halves = []
    for h in range(2):
        line = jnp.broadcast_to(rel[h : h + 1, :].astype(f32), tall).astype(bf16)
        parts = [
            jnp.where(line == (nodes + z).astype(bf16), one, zero) for z in range(0, wide, 16)
        ]
        halves.append(jnp.concatenate(parts, axis=0))
    return jnp.concatenate(halves, axis=1)


def list_visits(cells_ref, plan_ref, start_ref):
    blocks = cells_ref.shape[0] // 2
    shape = (blocks, LANES)
    number = lax.broadcasted_iota(jnp.int32, shape, 0)
    lane = lax.broadcasted_iota(jnp.int32, shape, 1)
    first_half = cells_ref[pl.ds(0, blocks, stride=2), :]
    second_half = cells_ref[pl.ds(1, blocks, stride=2), :]
    reached = jnp.maximum(
        jnp.where(first_half < LAST, first_half, 0), jnp.where(second_half < LAST, second_half, 0)
    )
    first = jnp.min(first_half, axis=1, keepdims=True)
    live = first < LAST
    last = jnp.max(reached, axis=1, keepdims=True)
    first_pair, last_pair = first >> 8, last >> 8
    start_ref[...] = jnp.broadcast_to(first_pair * WIDE, shape)
    pair = jnp.max(jnp.where(number == lane, first_pair, 0), axis=0, keepdims=True)
    plan_ref[0:1, :] = 2 * pair + (pair >> 4)
    within = live & (first_pair < lane) & (lane <= last_pair)
    block = jnp.max(jnp.where(within, number, -1), axis=0, keepdims=True)
    plan_ref[1:2, :] = jnp.maximum(block, 0)
    plan_ref[2:3, :] = jnp.where(block >= 0, lane[:1], PAIRS) * WIDE
    low = jnp.where(live, first_pair + number, 2 * LANES)
    high = jnp.where(live, last_pair + number, -1)
    inside = (low <= lane) & (lane <= high)
    block = jnp.max(jnp.where(inside, number, -1), axis=0, keepdims=True)
    valid = block >= 0
    pair = lane[:1] - block
    plan_ref[3:4, :] = jnp.where(valid, block, 0)
    plan_ref[4:5, :] = jnp.where(valid, 2 * pair + (pair >> 4), 0)
    plan_ref[5:6, :] = jnp.where(valid, pair, PAIRS) * WIDE
    plan_ref[6:7, :] = jnp.max(high, axis=0, keepdims=True) + 1
    plan_ref[7:8, :] = jnp.max(jnp.where(live, number + 1, 0), axis=0, keepdims=True)


def spread_kernel(
    frac_hbm, vel_hbm, mass_hbm, cells_hbm,
    far_ref, near_ref, layers_ref, plan_ref, frac_ref, vel_ref, cells_ref,
    listed_ref, start_ref, mass_ref, acc_ref, sems,
):
    slots = frac_ref.shape[1]
    sources = (cells_hbm, frac_hbm, vel_hbm, mass_hbm)
    targets = (cells_ref, frac_ref, vel_ref, mass_ref)
    arrivals = [
        pltpu.make_async_copy(source, target, sems.at[k])
        for k, (source, target) in enumerate(zip(sources, targets))
    ]
    for arrival in arrivals:
        arrival.start()
    acc_ref[...] = jnp.zeros_like(acc_ref)
    arrivals[0].wait()
    list_visits(cells_ref, plan_ref, start_ref)
    listing = pltpu.make_async_copy(plan_ref, listed_ref, sems.at[4])
    listing.start()
    for arrival in arrivals[1:]:
        arrival.wait()
    sublane = lax.broadcasted_iota(jnp.int32, (8, LANES), 0)
    lane = lax.broadcasted_iota(jnp.int32, (1, LANES), 1)
    top_z = sublane >= 4
    field = sublane & 3

    def weigh(part):
        at = pl.multiple_of(part * LANES, LANES)
        here = pl.ds(at, LANES)

        def spread_out(line):
            return jnp.broadcast_to(line, (8, LANES))

        fx, fy, fz = (spread_out(frac_ref[d : d + 1, here]) for d in range(3))
        vx, vy, vz = (spread_out(vel_ref[d : d + 1, here]) for d in range(3))
        live = cells_ref[pl.ds(part, 1), :] < LAST
        held = spread_out(jnp.where(live, mass_ref[pl.ds(part, 1), :], 0.0))
        carried = jnp.where(
            field == 0, held, held * jnp.where(field == 1, vx, jnp.where(field == 2, vy, vz))
        )
        carried = carried * jnp.where(top_z, fz, 1.0 - fz)
        lower, upper = carried * (1.0 - fx), carried * fx
        rows = jnp.concatenate(
            [lower * (1.0 - fy), lower * fy, upper * (1.0 - fy), upper * fy], axis=0
        )
        return jnp.concatenate(split_pair(rows), axis=0)

    def spread_one(block, offset):
        rel = relative(cells_ref, block, offset)
        row = (rel >> 7).astype(f32)
        shares = ([], [])
        for h in range(2):
            values = weigh(2 * block + h)
            which = jnp.broadcast_to(row[h : h + 1, :], values.shape).astype(bf16)
            for r in range(2):
                here = which == jnp.full(values.shape, r, bf16)
                shares[r].append(jnp.where(here, values, jnp.zeros_like(values)))
        both = lax.dot_general(
            jnp.concatenate([jnp.concatenate(share, axis=1) for share in shares], axis=0),
            one_hot(rel & (NZ - 1), NZ),
            (((1,), (1,)), ((), ())),
            preferred_element_type=f32,
        )
        first = both[:SPREAD] + both[SPREAD : 2 * SPREAD]
        second = both[2 * SPREAD : 3 * SPREAD] + both[3 * SPREAD :]
        return (
            jnp.concatenate([first[0:8], first[8:16] + second[0:8], second[8:16]], axis=0),
            jnp.concatenate([first[16:24], first[24:32] + second[16:24], second[24:32]], axis=0),
        )

    def add_to_nodes(base, parts):
        here = pl.ds(pl.multiple_of(base * 8, 8), 24)
        above = pl.ds(pl.multiple_of(base * 8, 8) + (NY + 1) * 8, 24)
        lower, upper = acc_ref[here, :], acc_ref[above, :]
        acc_ref[here, :] = lower + parts[0]
        acc_ref[above, :] = upper + parts[1]

    def first_pairs(group, carry):
        blocks = [group * GIVEN + u for u in range(GIVEN)]
        found = [spread_one(block, start_ref[pl.ds(block, 1), :]) for block in blocks]
        if carry is None:
            listing.wait()
        for block, parts in zip(blocks, found):
            add_to_nodes(listed_ref[0, block], parts)
        return carry

    first_pairs(0, None)
    found = [spread_one(listed_ref[1, pair], listed_ref[2, pair]) for pair in range(PAIRS)]
    for pair, parts in enumerate(found):
        add_to_nodes(2 * pair + (pair >> 4), parts)
    lax.fori_loop(1, (listed_ref[7, 0] + GIVEN - 1) // GIVEN, first_pairs, 0)

    odd = lax.axis_index("gx") % 2 == 1
    layers = []
    for l in range(CX + 1):
        first = l * (NY + 1) * 8
        acc_ref[first : first + 8, :] += acc_ref[first + NY * 8 : first + NY * 8 + 8, :]
        for f in range(4):
            lower = acc_ref[pl.ds(first + f, NY, stride=8), :]
            upper = acc_ref[pl.ds(first + 4 + f, NY, stride=8), :]
            layers.append(lower + pltpu.roll(upper, 1, 1))
            layers_ref[l * 4 + f] = layers[-1]
    for k in range(CX * 4):
        far_ref[k] = jnp.where(odd, layers[k + 4], layers[k])
        near_ref[k] = jnp.where(odd, layers[k], layers[k + 4])


def pair_up(field, axis):
    return field + pltpu.roll(field, field.shape[axis] - 1, axis)


def step_up(field, axis):
    return pltpu.roll(field, field.shape[axis] - 1, axis) - field


def pair_down(field, axis):
    return field + pltpu.roll(field, 1, axis)


def step_down(field, axis):
    return field - pltpu.roll(field, 1, axis)


def cell_stress(vel_lo, vel_hi, mass_lo, mass_hi, keep):
    grads = []
    for a in range(3):
        diff = vel_hi[a] - vel_lo[a]
        both = vel_hi[a] + vel_lo[a]
        grads.append(
            [
                0.25 * pair_up(pair_up(diff, 0), 1),
                0.25 * pair_up(step_up(both, 0), 1),
                0.25 * step_up(pair_up(both, 0), 1),
            ]
        )
    density = 0.125 * pair_up(pair_up(mass_hi + mass_lo, 0), 1)
    dxx = grads[0][0]
    dyy = grads[1][1]
    dzz = grads[2][2]
    dxy = 0.5 * (grads[0][1] + grads[1][0])
    dxz = 0.5 * (grads[0][2] + grads[2][0])
    dyz = 0.5 * (grads[1][2] + grads[2][1])
    second = dxx * dxx + dyy * dyy + dzz * dzz + 2.0 * (dxy * dxy + dxz * dxz + dyz * dyz)
    rate = jnp.sqrt(2.0 * second + rate_floor * rate_floor)
    pressure = stiffness * density
    inertial = rate * grain_size / jnp.sqrt(pressure + press_floor)
    friction = mu_static + (mu_limit - mu_static) * inertial / (inertia_ref + inertial)
    twice = 2.0 * friction * pressure / rate
    sigma = [
        twice * dxx - pressure,
        twice * dyy - pressure,
        twice * dzz - pressure,
        twice * dxy,
        twice * dxz,
        twice * dyz,
    ]
    return [jnp.where(keep, s, 0.0) for s in sigma]


def node_force(lower, upper):
    force = []
    for a in range(3):
        sx, sy, sz = (components[a][b] for b in range(3))
        along = pair_down(pair_down(upper[sx] - lower[sx], 0), 1)
        across = step_down(pair_down(upper[sy] + lower[sy], 1), 0)
        upward = step_down(pair_down(upper[sz] + lower[sz], 0), 1)
        force.append(0.25 * (along + across + upward))
    return force


def collect_kernel(
    step_ref, count_ref, plan_ref, layers_ref, far_new_ref, near_new_ref, frac_ref, vel_ref, cells_ref,
    out_ref, top_ref, listed_ref, tab_ref, pair_ref, sem,
):
    blocks = frac_ref.shape[1] // BLOCK
    listing = pltpu.make_async_copy(plan_ref, listed_ref, sem)
    listing.start()
    step = step_ref[0]
    odd = lax.axis_index("gx") % 2 == 1

    def pick(if_odd, if_even):
        return [jnp.where(odd, if_odd[k], if_even[k]) for k in range(4 * CX)]

    own = [layers_ref[k] for k in range(4 * (CX + 1))]
    left, right = pick(near_new_ref, far_new_ref), pick(far_new_ref, near_new_ref)
    nodes = [
        left[:4],
        [own[f] + left[4 + f] for f in range(4)],
        own[4:8],
        [own[8 + f] + right[f] for f in range(4)],
        right[4:],
    ]
    height = lax.broadcasted_iota(jnp.int32, (NY, NZ), 1)
    keep = height < NZ - 1
    above_bed = height > 0
    floor = [jnp.maximum(layer[0], mass_floor) for layer in nodes]
    v_old = [[layer[1 + a] / floor[l] for a in range(3)] for l, layer in enumerate(nodes)]
    sigma = [
        cell_stress(v_old[l], v_old[l + 1], nodes[l][0], nodes[l + 1][0], keep) for l in range(4)
    ]
    blank = jnp.zeros((NY, NZ), f32)
    for l in range(CX + 1):
        force = node_force(sigma[l], sigma[l + 1])
        fields = [blank] * 8
        for a in range(3):
            layer = nodes[l + 1]
            fresh = (layer[1 + a] + step * (force[a] + layer[0] * gravity[a])) / floor[l + 1]
            fresh = jnp.where(above_bed, fresh, 0.0)
            fields[a] = fresh - flip_share * v_old[l + 1][a]
            fields[4 + a] = step * fresh
        for k, value in enumerate(fields):
            start = l * NY * TABLE + k
            tab_ref[pl.ds(start, NY, stride=TABLE), :] = value
            tab_ref[pl.ds(start + 8, NY, stride=TABLE), :] = pltpu.roll(value, NZ - 1, 1)

    for l in range(CX + 1):

        def split_row(j, carry):
            at = pl.ds(pl.multiple_of((l * NY + j) * TABLE, TABLE), TABLE)
            high, low = split_pair(tab_ref[at, :])
            pair_ref[pl.ds(l * (NY + 1) + j, 1)] = jnp.concatenate([high, low], axis=0)[None]
            return carry

        lax.fori_loop(0, NY, split_row, 0, unroll=8)
        pair_ref[l * (NY + 1) + NY] = pair_ref[l * (NY + 1)]

    out_ref[...] = jnp.zeros_like(out_ref)
    listing.wait()
    total = listed_ref[6, 0]
    count = count_ref[0]
    lane = lax.broadcasted_iota(jnp.int32, (2, LANES), 1)
    half = lax.broadcasted_iota(jnp.int32, (2, LANES), 0)

    def visit(group, top):
        found = []
        for u in range(TAKEN):
            v = group * TAKEN + u
            block = listed_ref[3, v]
            base = listed_ref[4, v]
            rel = relative(cells_ref, block, listed_ref[5, v])
            hot = one_hot(rel, WIDE)
            rows = []
            for a in range(2):
                three = [pair_ref[base + a * (NY + 1) + k] for k in range(3)]
                rows += [jnp.concatenate(three[b : b + 2], axis=1) for b in range(2)]
            both = jnp.dot(jnp.concatenate(rows, axis=0), hot, preferred_element_type=f32)
            corners = []
            for k in range(4):
                four = both[2 * TABLE * k : 2 * TABLE * (k + 1)]
                corners += [four[0:8] + four[16:24], four[8:16] + four[24:32]]
            here = pl.ds(pl.multiple_of(block * BLOCK, BLOCK), BLOCK)
            frac = frac_ref[:, here]
            for d in (2, 1, 0):
                share = frac[d : d + 1, :]
                corners = [
                    corners[k] + share * (corners[k + 1] - corners[k])
                    for k in range(0, len(corners), 2)
                ]
            fresh = flip_share * vel_ref[:, here] + corners[0][0:3]
            square = jnp.sum(fresh * fresh, axis=0, keepdims=True)
            slot = block * BLOCK + half * LANES + lane
            taken = (rel >= 0) & (rel < WIDE) & (slot < count)
            for h in range(2):
                part = square[:, h * LANES : (h + 1) * LANES]
                top = jnp.maximum(top, jnp.where(taken[h : h + 1], part, 0.0))
            found.append((block, corners[0]))
        for block, part in found:
            out_ref[pl.ds(block, 1)] += part[None]
        return top

    top = jnp.zeros((1, LANES), f32)
    for group in range(2):
        top = visit(group, top)
    top = lax.fori_loop(2, (total + TAKEN - 1) // TAKEN, visit, top)
    top = jnp.sqrt(jnp.max(top, axis=1, keepdims=True))
    top_ref[...] = jnp.broadcast_to(top, top_ref.shape)


def finish_kernel(cells_ref, moved_ref, frac_ref, vel_ref, new_frac_ref, new_vel_ref):
    blocks = frac_ref.shape[1] // BLOCK

    def finish(block, carry):
        at = pl.multiple_of(block * BLOCK, BLOCK)
        here = pl.ds(at, BLOCK)
        cells = cells_ref[pl.ds(block * 2, 2), :]
        alive = jnp.concatenate([cells[0:1], cells[1:2]], axis=1) < LAST
        got = moved_ref[pl.ds(block, 1)][0]
        new_vel_ref[:, here] = jnp.where(alive, flip_share * vel_ref[:, here] + got[0:3], 0.0)
        new_frac_ref[:, here] = jnp.where(alive, frac_ref[:, here] + got[4:7], 0.0)
        return carry

    lax.fori_loop(0, blocks, finish, 0, unroll=4)


def largest(value, axis):
    devices = lax.axis_size(axis)
    reach = 1
    while reach < devices:
        if devices & (devices - 1) == 0:
            pairs = [(i, i ^ (reach | 1)) for i in range(devices)]
        else:
            pairs = [(i, (i + reach) % devices) for i in range(devices)]
        value = jnp.maximum(value, lax.ppermute(value, axis, pairs))
        reach *= 2
    return value


smem = pl.BlockSpec(memory_space=pltpu.SMEM)
vmem = pl.BlockSpec(memory_space=pltpu.VMEM)
hbm = pl.BlockSpec(memory_space=pltpu.HBM)


def body(frac, velocity, mass, particle_cell, tile_count, time_step):
    slots = frac.shape[1]
    blocks = slots // BLOCK
    rows = slots // LANES
    inputs = (frac, velocity, mass.reshape(rows, LANES), particle_cell.reshape(rows, LANES))
    far, near, layers, plan, frac_here, vel_here, cells_here = pl.pallas_call(
        spread_kernel,
        out_shape=(
            pltpu.VMEM((4 * CX, NY, NZ), f32),
            pltpu.VMEM((4 * CX, NY, NZ), f32),
            pltpu.VMEM((4 * (CX + 1), NY, NZ), f32),
            pltpu.VMEM((8, LANES), jnp.int32),
            pltpu.VMEM(frac.shape, f32),
            pltpu.VMEM(velocity.shape, f32),
            pltpu.VMEM((rows, LANES), jnp.int32),
        ),
        in_specs=[hbm] * 4,
        out_specs=(vmem,) * 7,
        scratch_shapes=[
            pltpu.SMEM((8, LANES), jnp.int32),
            pltpu.VMEM((blocks, LANES), jnp.int32),
            pltpu.VMEM((rows, LANES), f32),
            pltpu.VMEM(((CX + 1) * (NY + 1) * 8, NZ), f32),
            pltpu.SemaphoreType.DMA((5,)),
        ],
        compiler_params=pltpu.CompilerParams(vmem_limit_bytes=32 * 1024 * 1024),
        name="spread",
    )(*[pltpu.with_memory_space_constraint(x, pltpu.HBM) for x in inputs])
    devices = lax.axis_size("gx")
    far_pairs = [(i, (i + (1 if i % 2 else -1)) % devices) for i in range(devices)]
    near_pairs = [(i, i ^ 1) for i in range(devices)]
    far_new = lax.ppermute(far, "gx", far_pairs)
    near_new = lax.ppermute(near, "gx", near_pairs)
    moved, top = pl.pallas_call(
        collect_kernel,
        out_shape=(
            jax.ShapeDtypeStruct((blocks, 8, BLOCK), f32),
            jax.ShapeDtypeStruct((8, LANES), f32),
        ),
        in_specs=[smem] * 2 + [vmem] * 7,
        out_specs=(vmem, vmem),
        scratch_shapes=[
            pltpu.SMEM((8, LANES), jnp.int32),
            pltpu.VMEM(((CX + 1) * NY * TABLE, NZ), f32),
            pltpu.VMEM(((CX + 1) * (NY + 1), 2 * TABLE, NZ), bf16),
            pltpu.SemaphoreType.DMA,
        ],
        compiler_params=pltpu.CompilerParams(vmem_limit_bytes=32 * 1024 * 1024),
        name="collect",
    )(time_step, tile_count, plan, layers, far_new, near_new, frac_here, vel_here, cells_here)
    new_frac, new_velocity = pl.pallas_call(
        finish_kernel,
        out_shape=(
            jax.ShapeDtypeStruct(frac.shape, f32),
            jax.ShapeDtypeStruct(velocity.shape, f32),
        ),
        in_specs=[vmem] * 4,
        out_specs=(vmem, vmem),
        compiler_params=pltpu.CompilerParams(vmem_limit_bytes=32 * 1024 * 1024),
        cost_estimate=pl.CostEstimate(flops=0, bytes_accessed=8000000, transcendentals=0),
        name="finish",
    )(cells_here, moved, frac_here, vel_here)
    fastest = largest(top, "gx")
    next_step = (courant / (fastest + wave_speed))[0, :1]
    return (new_frac, new_velocity, next_step)


def solution(mesh):
    placed = (
        P(None, ("runs", "gx")),
        P(None, ("runs", "gx")),
        P(("runs", "gx")),
        P(("runs", "gx")),
        P(("runs", "gx")),
        P("runs"),
    )
    return jax.shard_map(
        body,
        mesh=mesh,
        in_specs=placed,
        out_specs=(P(None, ("runs", "gx")), P(None, ("runs", "gx")), P("runs")),
        check_vma=False,
    )
```

profile of v0, /device:TPU:0, one launch (start us, length us, event | category | flops | bytes accessed | tf_op | source)
XLA Modules:
  0.0 28.1 jit_solution(4893234748947312671)
XLA Ops:
  0.6 3.9 %spread.1 = (f32[8,32,128]{2,1,0:T(8,128)S(1)}, f32[8,32,128]{2,1,0:T(8,128)S(1)}, f32[12,32,128]{2,1,0:T(8,128)S(1)}, s32[8,128]{1,0:T(8,128)S(1)}, f32[3,16384...) custom-call(f32[3,16384]{1,0:T(4,128)} %frac_hbm.1, f32[3,16384]{1,0:T(4,128)} %vel_hbm.1, ...), custom_call_target="tpu_custom_call" | custom-call | tf_op jit(solution)/shard_map/spread/pallas_call | solution.py:416
  4.5 5.5 %collective-permute-start = (f32[8,32,128]{2,1,0:T(8,128)S(1)}, f32[8,32,128]{2,1,0:T(8,128)S(1)}, u32[]{:S(2)}, u32[]{:S(2)}) collective-permute-start(f32[8,32,128]{2,1,0:T(8,128)S(1)} %get-tuple-element.17), channel_id=1, source_target_pairs={{0,15},{1,2},{2,1},{3,4},{4,3},{5,6},{6,5},{7,8},{8,7},{9,10},{10,... | collective-permute-start | bytes 393224 | tf_op jit(solution)/shard_map/ppermute | solution.py:442
  10.0 0.0 collective-permute-start.1
  11.3 1.4 %collective-permute-done.far_new_ref = f32[8,32,128]{2,1,0:T(8,128)S(1)} collective-permute-done((f32[8,32,128]{2,1,0:T(8,128)S(1)}, f32[8,32,128]{2,1,0:T(8,128)S(1)}, u32[]{:S(2)}, u32[]{:S(2)}) %collective-permute-start) | collective-permute-done | bytes 131104 | tf_op jit(solution)/shard_map/ppermute | solution.py:442
  12.6 0.0 collective-permute-done.1.near_new_ref
  12.6 3.7 %collect.1 = (f32[64,8,256]{2,1,0:T(8,128)S(1)}, f32[8,128]{1,0:T(8,128)S(1)}) custom-call(f32[1]{0:T(128)S(6)} %copy.10.step_ref, s32[1]{0:T(128)S(6)} %copy.9.count_ref, s32[8,128]{1,0:T(8,128)S(1)} %get-tuple-element.15.plan_ref, f32[12,32,128]{2,1,0:T(8,128)S(1)} %get-tuple-element.16.layers_ref, f32[8,32,128]{2,1,0:T(8,128)S(1)} %collective-permute-done.far_new_ref, ...), custom_call_target="tpu_custom_call" | custom-call | tf_op jit(solution)/shard_map/collect/pallas_call | solution.py:444
  16.4 0.1 collective-permute-start.2
  16.4 1.2 %collective-permute-done.2 = f32[8,128]{1,0:T(8,128)S(1)} collective-permute-done((f32[8,128]{1,0:T(8,128)S(1)}, f32[8,128]{1,0:T(8,128)S(1)}, u32[]{:S(2)}, u32[]{:S(2)}) %collective-permute-start.2) | collective-permute-done | bytes 4128 | tf_op jit(solution)/shard_map/ppermute | solution.py:401
  17.6 0.0 collective-permute-start.3
  17.6 3.0 %collective-permute-done.3 = f32[8,128]{1,0:T(8,128)S(1)} collective-permute-done((f32[8,128]{1,0:T(8,128)S(1)}, f32[8,128]{1,0:T(8,128)S(1)}, u32[]{:S(2)}, u32[]{:S(2)}) %collective-permute-start.3) | collective-permute-done | bytes 4128 | tf_op jit(solution)/shard_map/ppermute | solution.py:401
  20.6 0.0 collective-permute-start.4
  20.6 3.0 %collective-permute-done.4 = f32[8,128]{1,0:T(8,128)S(1)} collective-permute-done((f32[8,128]{1,0:T(8,128)S(1)}, f32[8,128]{1,0:T(8,128)S(1)}, u32[]{:S(2)}, u32[]{:S(2)}) %collective-permute-start.4) | collective-permute-done | bytes 4128 | tf_op jit(solution)/shard_map/ppermute | solution.py:401
  23.7 1.8 %collective-permute-start.5 = (f32[8,128]{1,0:T(8,128)S(1)}, f32[8,128]{1,0:T(8,128)S(1)}, u32[]{:S(2)}, u32[]{:S(2)}) collective-permute-start(f32[8,128]{1,0:T(8,128)S(1)} %max.14), channel_id=1, source_target_pairs={{0,9},{1,8},{2,11},{3,10},{4,13},{5,12},{6,15},{7,14},{8,1},{9,0},... | collective-permute-start | bytes 12296 | tf_op jit(solution)/shard_map/ppermute | solution.py:401
  25.5 1.1 %finish.1 = (f32[3,16384]{1,0:T(4,128)}, f32[3,16384]{1,0:T(4,128)}) custom-call(s32[128,128]{1,0:T(8,128)S(1)} %get-tuple-element.14.cells_ref, f32[64,8,256]{2,1,0:T(8,128)S(1)} %get-tuple-element.21.moved_ref, f32[3,16384]{1,0:T(4,128)S(1)} %get-tuple-element.19.frac_ref, f32[3,16384]{1,0:T(4,128)S(1)} %get-tuple-element.20.vel_ref), custom_call_target="tpu_custom_call" | custom-call | bytes 8000000 | tf_op jit(solution)/shard_map/finish/pallas_call | solution.py:461
  26.6 1.0 %collective-permute-done.5 = f32[8,128]{1,0:T(8,128)S(1)} collective-permute-done((f32[8,128]{1,0:T(8,128)S(1)}, f32[8,128]{1,0:T(8,128)S(1)}, u32[]{:S(2)}, u32[]{:S(2)}) %collective-permute-start.5) | collective-permute-done | bytes 4128 | tf_op jit(solution)/shard_map/ppermute | solution.py:401
  27.6 0.5 %slice.3 = f32[1,1]{1,0:T(1,128)} slice(f32[8,128]{1,0:T(8,128)S(1)} %add_divide_fusion), slice={[0:1], [0:1]} | slice | bytes 8 | tf_op jit(solution)/shard_map/slice | solution.py:474
  (4 shorter events, 0.0 us)
Async XLA Ops:
  4.5 8.2 %collective-permute-start = (f32[8,32,128]{2,1,0:T(8,128)S(1)}, f32[8,32,128]{2,1,0:T(8,128)S(1)}, u32[]{:S(2)}, u32[]{:S(2)}) collective-permute-start(f32[8,32,128]{2,1,0:T(8,128)S(1)} %get-tuple-element.17), channel_id=1, source_target_pairs={{0,15},{1,2},{2,1},{3,4},{4,3},{5,6},{6,5},{7,8},{8,7},{9,10},{10,... | collective-permute-start | bytes 393224 | tf_op jit(solution)/shard_map/ppermute | solution.py:442
  10.0 2.7 %collective-permute-start.1 = (f32[8,32,128]{2,1,0:T(8,128)S(1)}, f32[8,32,128]{2,1,0:T(8,128)S(1)}, u32[]{:S(2)}, u32[]{:S(2)}) collective-permute-start(f32[8,32,128]{2,1,0:T(8,128)S(1)} %get-tuple-element.18), channel_id=1, source_target_pairs={{0,1},{1,0},{2,3},{3,2},{4,5},{5,4},{6,7},{7,6},{8,9},{9,8},{10,11... | collective-permute-start | bytes 393224 | tf_op jit(solution)/shard_map/ppermute | solution.py:443
  16.4 1.2 %collective-permute-start.2 = (f32[8,128]{1,0:T(8,128)S(1)}, f32[8,128]{1,0:T(8,128)S(1)}, u32[]{:S(2)}, u32[]{:S(2)}) collective-permute-start(f32[8,128]{1,0:T(8,128)S(1)} %get-tuple-element.24), channel_id=1, source_target_pairs={{0,1},{1,0},{2,3},{3,2},{4,5},{5,4},{6,7},{7,6},{8,9},{9,8},{10,11... | collective-permute-start | bytes 12296 | tf_op jit(solution)/shard_map/ppermute | solution.py:401
  17.6 3.0 %collective-permute-start.3 = (f32[8,128]{1,0:T(8,128)S(1)}, f32[8,128]{1,0:T(8,128)S(1)}, u32[]{:S(2)}, u32[]{:S(2)}) collective-permute-start(f32[8,128]{1,0:T(8,128)S(1)} %max.12), channel_id=1, source_target_pairs={{0,3},{1,2},{2,1},{3,0},{4,7},{5,6},{6,5},{7,4},{8,11},{9,10},{10,... | collective-permute-start | bytes 12296 | tf_op jit(solution)/shard_map/ppermute | solution.py:401
  20.6 3.0 %collective-permute-start.4 = (f32[8,128]{1,0:T(8,128)S(1)}, f32[8,128]{1,0:T(8,128)S(1)}, u32[]{:S(2)}, u32[]{:S(2)}) collective-permute-start(f32[8,128]{1,0:T(8,128)S(1)} %max.13), channel_id=1, source_target_pairs={{0,5},{1,4},{2,7},{3,6},{4,1},{5,0},{6,3},{7,2},{8,13},{9,12},{10,... | collective-permute-start | bytes 12296 | tf_op jit(solution)/shard_map/ppermute | solution.py:401
  23.7 3.9 %collective-permute-start.5 = (f32[8,128]{1,0:T(8,128)S(1)}, f32[8,128]{1,0:T(8,128)S(1)}, u32[]{:S(2)}, u32[]{:S(2)}) collective-permute-start(f32[8,128]{1,0:T(8,128)S(1)} %max.14), channel_id=1, source_target_pairs={{0,9},{1,8},{2,11},{3,10},{4,13},{5,12},{6,15},{7,14},{8,1},{9,0},... | collective-permute-start | bytes 12296 | tf_op jit(solution)/shard_map/ppermute | solution.py:401
where the time goes:
time: 28.3 us; the launch traced here: 28.1 us
  waiting for transfers between devices  9.58 us (34%)
  Pallas kernels  8.64 us (31%)
  starting transfers between devices  7.42 us (26%)
  between operations  1.96 us (7%)
  local copies, waits for them, and re-layouts  0.52 us (2%)
    ppermute x4, waiting for transfers between devices, largest(): value = jnp.maximum(value, lax.ppermute(value, axis, pairs))  8.22 us
    ppermute x1, starting transfers between devices, body(): far_new = lax.ppermute(far, 'gx', far_pairs)  5.5 us
    pallas_call x1, Pallas kernels, body(): pl.pallas_call(spread_kernel, out_shape=(pltpu.VMEM((4 * CX, NY, NZ), f32...  3.85 us
    pallas_call x1, Pallas kernels, body(): pl.pallas_call(collect_kernel, out_shape=(jax.ShapeDtypeStruct((blocks, 8...  3.72 us
    ppermute x4, starting transfers between devices, largest(): value = jnp.maximum(value, lax.ppermute(value, axis, pairs))  1.92 us
    ppermute x1, waiting for transfers between devices, body(): far_new = lax.ppermute(far, 'gx', far_pairs)  1.35 us
    pallas_call x1, Pallas kernels, body(): pl.pallas_call(finish_kernel, out_shape=(jax.ShapeDtypeStruct(frac.shape,...  1.08 us
  transfers between devices with their start and end apart: 6, of which 5 were waited for; matrix products, arithmetic and copies ran while one was open for 0% of the time, Pallas kernels for 4%

commit v1 on v0

--- a/solution.py
+++ b/solution.py
@@ -14,6 +14,7 @@
 PAIRS = ROWS // 2
 LAST = ROWS * NZ - 1
 WIDE = 2 * NZ
+TALL = 4
 BLOCK = 256
 LANES = 128
 GIVEN = 32
@@ -75,14 +76,15 @@
     first = jnp.min(first_half, axis=1, keepdims=True)
     live = first < LAST
     last = jnp.max(reached, axis=1, keepdims=True)
-    first_pair, last_pair = first >> 8, last >> 8
-    start_ref[...] = jnp.broadcast_to(first_pair * WIDE, shape)
-    pair = jnp.max(jnp.where(number == lane, first_pair, 0), axis=0, keepdims=True)
-    plan_ref[0:1, :] = 2 * pair + (pair >> 4)
-    within = live & (first_pair < lane) & (lane <= last_pair)
+    first_four, last_four = first >> 9, last >> 9
+    start_ref[...] = jnp.broadcast_to(first_four * (TALL * NZ), shape)
+    four = jnp.max(jnp.where(number == lane, first_four, 0), axis=0, keepdims=True)
+    plan_ref[0:1, :] = TALL * four + (four >> 3)
+    within = live & (first_four < lane) & (lane <= last_four)
     block = jnp.max(jnp.where(within, number, -1), axis=0, keepdims=True)
     plan_ref[1:2, :] = jnp.maximum(block, 0)
-    plan_ref[2:3, :] = jnp.where(block >= 0, lane[:1], PAIRS) * WIDE
+    plan_ref[2:3, :] = jnp.where(block >= 0, lane[:1] * TALL, ROWS) * NZ
+    first_pair, last_pair = first >> 8, last >> 8
     low = jnp.where(live, first_pair + number, 2 * LANES)
     high = jnp.where(live, last_pair + number, -1)
     inside = (low <= lane) & (lane <= high)
@@ -146,11 +148,11 @@
     def spread_one(block, offset):
         rel = relative(cells_ref, block, offset)
         row = (rel >> 7).astype(f32)
-        shares = ([], [])
+        shares = [[] for _ in range(TALL)]
         for h in range(2):
             values = weigh(2 * block + h)
             which = jnp.broadcast_to(row[h : h + 1, :], values.shape).astype(bf16)
-            for r in range(2):
+            for r in range(TALL):
                 here = which == jnp.full(values.shape, r, bf16)
                 shares[r].append(jnp.where(here, values, jnp.zeros_like(values)))
         both = lax.dot_general(
@@ -159,21 +161,25 @@
             (((1,), (1,)), ((), ())),
             preferred_element_type=f32,
         )
-        first = both[:SPREAD] + both[SPREAD : 2 * SPREAD]
-        second = both[2 * SPREAD : 3 * SPREAD] + both[3 * SPREAD :]
-        return (
-            jnp.concatenate([first[0:8], first[8:16] + second[0:8], second[8:16]], axis=0),
-            jnp.concatenate([first[16:24], first[24:32] + second[16:24], second[24:32]], axis=0),
-        )
+        sums = []
+        for r in range(TALL):
+            at = 2 * SPREAD * r
+            sums.append(both[at : at + SPREAD] + both[at + SPREAD : at + 2 * SPREAD])
+        parts = []
+        for a in (0, 16):
+            lines = [sums[0][a : a + 8]]
+            lines += [sums[r - 1][a + 8 : a + 16] + sums[r][a : a + 8] for r in range(1, TALL)]
+            parts.append(jnp.concatenate(lines + [sums[-1][a + 8 : a + 16]], axis=0))
+        return parts
 
     def add_to_nodes(base, parts):
-        here = pl.ds(pl.multiple_of(base * 8, 8), 24)
-        above = pl.ds(pl.multiple_of(base * 8, 8) + (NY + 1) * 8, 24)
+        here = pl.ds(pl.multiple_of(base * 8, 8), (TALL + 1) * 8)
+        above = pl.ds(pl.multiple_of(base * 8, 8) + (NY + 1) * 8, (TALL + 1) * 8)
         lower, upper = acc_ref[here, :], acc_ref[above, :]
         acc_ref[here, :] = lower + parts[0]
         acc_ref[above, :] = upper + parts[1]
 
-    def first_pairs(group, carry):
+    def first_fours(group, carry):
         blocks = [group * GIVEN + u for u in range(GIVEN)]
         found = [spread_one(block, start_ref[pl.ds(block, 1), :]) for block in blocks]
         if carry is None:
@@ -182,11 +188,11 @@
             add_to_nodes(listed_ref[0, block], parts)
         return carry
 
-    first_pairs(0, None)
-    found = [spread_one(listed_ref[1, pair], listed_ref[2, pair]) for pair in range(PAIRS)]
-    for pair, parts in enumerate(found):
-        add_to_nodes(2 * pair + (pair >> 4), parts)
-    lax.fori_loop(1, (listed_ref[7, 0] + GIVEN - 1) // GIVEN, first_pairs, 0)
+    first_fours(0, None)
+    found = [spread_one(listed_ref[1, k], listed_ref[2, k]) for k in range(ROWS // TALL)]
+    for k, parts in enumerate(found):
+        add_to_nodes(TALL * k + (k >> 3), parts)
+    lax.fori_loop(1, (listed_ref[7, 0] + GIVEN - 1) // GIVEN, first_fours, 0)
 
     odd = lax.axis_index("gx") % 2 == 1
     layers = []

time: 28.3 us -> 28.8 us (1.018); the launches traced: 28.1 us -> 28.3 us
  starting transfers between devices: 7.42 us -> 11.3 us
  waiting for transfers between devices: 9.58 us -> 7.18 us
  Pallas kernels: 8.64 us -> 7.32 us
    ppermute x4, starting transfers between devices: 1.92 us -> 4.47 us  [largest(): value = jnp.maximum(value, lax.ppermute(value, axis, pairs))]
    ppermute x4, waiting for transfers between devices: 8.22 us -> 5.82 us  [largest(): value = jnp.maximum(value, lax.ppermute(value, axis, pairs))]
    ppermute x1, starting transfers between devices: 5.5 us -> 6.82 us  [body(): far_new = lax.ppermute(far, 'gx', far_pairs)]
    pallas_call x1, Pallas kernels: 3.72 us -> 2.81 us  [body(): pl.pallas_call(collect_kernel, out_shape=(jax.ShapeDtypeStruct((blocks, 8...]
    pallas_call x1, Pallas kernels: 3.85 us -> 3.43 us  [body(): pl.pallas_call(spread_kernel, out_shape=(pltpu.VMEM((4 * CX, NY, NZ), f32...]
where the time goes in v1:
time: 28.8 us; the launch traced here: 28.3 us
  starting transfers between devices  11.3 us (39%)
  Pallas kernels  7.32 us (25%)
  waiting for transfers between devices  7.18 us (25%)
  between operations  1.96 us (7%)
  local copies, waits for them, and re-layouts  0.52 us (2%)
    ppermute x1, starting transfers between devices, body(): far_new = lax.ppermute(far, 'gx', far_pairs)  6.82 us
    ppermute x4, waiting for transfers between devices, largest(): value = jnp.maximum(value, lax.ppermute(value, axis, pairs))  5.82 us
    ppermute x4, starting transfers between devices, largest(): value = jnp.maximum(value, lax.ppermute(value, axis, pairs))  4.47 us
    pallas_call x1, Pallas kernels, body(): pl.pallas_call(spread_kernel, out_shape=(pltpu.VMEM((4 * CX, NY, NZ), f32...  3.43 us
    pallas_call x1, Pallas kernels, body(): pl.pallas_call(collect_kernel, out_shape=(jax.ShapeDtypeStruct((blocks, 8...  2.81 us
    ppermute x1, waiting for transfers between devices, body(): far_new = lax.ppermute(far, 'gx', far_pairs)  1.35 us
    pallas_call x1, Pallas kernels, body(): pl.pallas_call(finish_kernel, out_shape=(jax.ShapeDtypeStruct(frac.shape,...  1.08 us
  transfers between devices with their start and end apart: 6, of which 5 were waited for; matrix products, arithmetic and copies ran while one was open for 0% of the time, Pallas kernels for 4%

profile of v1, /device:TPU:0, one launch (start us, length us, event | category | flops | bytes accessed | tf_op | source)
XLA Modules:
  0.0 28.3 jit_solution(15602572734958025796)
XLA Ops:
  0.6 3.4 %spread.1 = (f32[8,32,128]{2,1,0:T(8,128)S(1)}, f32[8,32,128]{2,1,0:T(8,128)S(1)}, f32[12,32,128]{2,1,0:T(8,128)S(1)}, s32[8,128]{1,0:T(8,128)S(1)}, f32[3,16384...) custom-call(f32[3,16384]{1,0:T(4,128)} %frac_hbm.1, f32[3,16384]{1,0:T(4,128)} %vel_hbm.1, ...), custom_call_target="tpu_custom_call" | custom-call | tf_op jit(solution)/shard_map/spread/pallas_call | solution.py:422
  4.1 6.8 %collective-permute-start = (f32[8,32,128]{2,1,0:T(8,128)S(1)}, f32[8,32,128]{2,1,0:T(8,128)S(1)}, u32[]{:S(2)}, u32[]{:S(2)}) collective-permute-start(f32[8,32,128]{2,1,0:T(8,128)S(1)} %get-tuple-element.17), channel_id=1, source_target_pairs={{0,15},{1,2},{2,1},{3,4},{4,3},{5,6},{6,5},{7,8},{8,7},{9,10},{10,... | collective-permute-start | bytes 393224 | tf_op jit(solution)/shard_map/ppermute | solution.py:448
  10.9 0.0 collective-permute-start.1
  12.2 1.4 %collective-permute-done.far_new_ref = f32[8,32,128]{2,1,0:T(8,128)S(1)} collective-permute-done((f32[8,32,128]{2,1,0:T(8,128)S(1)}, f32[8,32,128]{2,1,0:T(8,128)S(1)}, u32[]{:S(2)}, u32[]{:S(2)}) %collective-permute-start) | collective-permute-done | bytes 131104 | tf_op jit(solution)/shard_map/ppermute | solution.py:448
  13.5 0.0 collective-permute-done.1.near_new_ref
  13.5 2.8 %collect.1 = (f32[64,8,256]{2,1,0:T(8,128)S(1)}, f32[8,128]{1,0:T(8,128)S(1)}) custom-call(f32[1]{0:T(128)S(6)} %copy.10.step_ref, s32[1]{0:T(128)S(6)} %copy.9.count_ref, s32[8,128]{1,0:T(8,128)S(1)} %get-tuple-element.15.plan_ref, f32[12,32,128]{2,1,0:T(8,128)S(1)} %get-tuple-element.16.layers_ref, f32[8,32,128]{2,1,0:T(8,128)S(1)} %collective-permute-done.far_new_ref, ...), custom_call_target="tpu_custom_call" | custom-call | tf_op jit(solution)/shard_map/collect/pallas_call | solution.py:450
  16.4 0.1 collective-permute-start.2
  16.4 1.2 %collective-permute-done.2 = f32[8,128]{1,0:T(8,128)S(1)} collective-permute-done((f32[8,128]{1,0:T(8,128)S(1)}, f32[8,128]{1,0:T(8,128)S(1)}, u32[]{:S(2)}, u32[]{:S(2)}) %collective-permute-start.2) | collective-permute-done | bytes 4128 | tf_op jit(solution)/shard_map/ppermute | solution.py:407
  17.6 0.5 %collective-permute-start.3 = (f32[8,128]{1,0:T(8,128)S(1)}, f32[8,128]{1,0:T(8,128)S(1)}, u32[]{:S(2)}, u32[]{:S(2)}) collective-permute-start(f32[8,128]{1,0:T(8,128)S(1)} %max.12), channel_id=1, source_target_pairs={{0,3},{1,2},{2,1},{3,0},{4,7},{5,6},{6,5},{7,4},{8,11},{9,10},{10,... | collective-permute-start | bytes 12296 | tf_op jit(solution)/shard_map/ppermute | solution.py:407
  18.1 2.5 %collective-permute-done.3 = f32[8,128]{1,0:T(8,128)S(1)} collective-permute-done((f32[8,128]{1,0:T(8,128)S(1)}, f32[8,128]{1,0:T(8,128)S(1)}, u32[]{:S(2)}, u32[]{:S(2)}) %collective-permute-start.3) | collective-permute-done | bytes 4128 | tf_op jit(solution)/shard_map/ppermute | solution.py:407
  20.6 1.1 %collective-permute-start.4 = (f32[8,128]{1,0:T(8,128)S(1)}, f32[8,128]{1,0:T(8,128)S(1)}, u32[]{:S(2)}, u32[]{:S(2)}) collective-permute-start(f32[8,128]{1,0:T(8,128)S(1)} %max.13), channel_id=1, source_target_pairs={{0,5},{1,4},{2,7},{3,6},{4,1},{5,0},{6,3},{7,2},{8,13},{9,12},{10,... | collective-permute-start | bytes 12296 | tf_op jit(solution)/shard_map/ppermute | solution.py:407
  21.8 1.9 %collective-permute-done.4 = f32[8,128]{1,0:T(8,128)S(1)} collective-permute-done((f32[8,128]{1,0:T(8,128)S(1)}, f32[8,128]{1,0:T(8,128)S(1)}, u32[]{:S(2)}, u32[]{:S(2)}) %collective-permute-start.4) | collective-permute-done | bytes 4128 | tf_op jit(solution)/shard_map/ppermute | solution.py:407
  23.7 2.8 %collective-permute-start.5 = (f32[8,128]{1,0:T(8,128)S(1)}, f32[8,128]{1,0:T(8,128)S(1)}, u32[]{:S(2)}, u32[]{:S(2)}) collective-permute-start(f32[8,128]{1,0:T(8,128)S(1)} %max.14), channel_id=1, source_target_pairs={{0,9},{1,8},{2,11},{3,10},{4,13},{5,12},{6,15},{7,14},{8,1},{9,0},... | collective-permute-start | bytes 12296 | tf_op jit(solution)/shard_map/ppermute | solution.py:407
  26.4 1.1 %finish.1 = (f32[3,16384]{1,0:T(4,128)}, f32[3,16384]{1,0:T(4,128)}) custom-call(s32[128,128]{1,0:T(8,128)S(1)} %get-tuple-element.14.cells_ref, f32[64,8,256]{2,1,0:T(8,128)S(1)} %get-tuple-element.21.moved_ref, f32[3,16384]{1,0:T(4,128)S(1)} %get-tuple-element.19.frac_ref, f32[3,16384]{1,0:T(4,128)S(1)} %get-tuple-element.20.vel_ref), custom_call_target="tpu_custom_call" | custom-call | bytes 8000000 | tf_op jit(solution)/shard_map/finish/pallas_call | solution.py:467
  27.5 0.3 collective-permute-done.5
  27.8 0.5 %slice.3 = f32[1,1]{1,0:T(1,128)} slice(f32[8,128]{1,0:T(8,128)S(1)} %add_divide_fusion), slice={[0:1], [0:1]} | slice | bytes 8 | tf_op jit(solution)/shard_map/slice | solution.py:480
  (4 shorter events, 0.0 us)
Async XLA Ops:
  4.1 9.5 %collective-permute-start = (f32[8,32,128]{2,1,0:T(8,128)S(1)}, f32[8,32,128]{2,1,0:T(8,128)S(1)}, u32[]{:S(2)}, u32[]{:S(2)}) collective-permute-start(f32[8,32,128]{2,1,0:T(8,128)S(1)} %get-tuple-element.17), channel_id=1, source_target_pairs={{0,15},{1,2},{2,1},{3,4},{4,3},{5,6},{6,5},{7,8},{8,7},{9,10},{10,... | collective-permute-start | bytes 393224 | tf_op jit(solution)/shard_map/ppermute | solution.py:448
  10.9 2.7 %collective-permute-start.1 = (f32[8,32,128]{2,1,0:T(8,128)S(1)}, f32[8,32,128]{2,1,0:T(8,128)S(1)}, u32[]{:S(2)}, u32[]{:S(2)}) collective-permute-start(f32[8,32,128]{2,1,0:T(8,128)S(1)} %get-tuple-element.18), channel_id=1, source_target_pairs={{0,1},{1,0},{2,3},{3,2},{4,5},{5,4},{6,7},{7,6},{8,9},{9,8},{10,11... | collective-permute-start | bytes 393224 | tf_op jit(solution)/shard_map/ppermute | solution.py:449
  16.4 1.2 %collective-permute-start.2 = (f32[8,128]{1,0:T(8,128)S(1)}, f32[8,128]{1,0:T(8,128)S(1)}, u32[]{:S(2)}, u32[]{:S(2)}) collective-permute-start(f32[8,128]{1,0:T(8,128)S(1)} %get-tuple-element.24), channel_id=1, source_target_pairs={{0,1},{1,0},{2,3},{3,2},{4,5},{5,4},{6,7},{7,6},{8,9},{9,8},{10,11... | collective-permute-start | bytes 12296 | tf_op jit(solution)/shard_map/ppermute | solution.py:407
  17.6 3.0 %collective-permute-start.3 = (f32[8,128]{1,0:T(8,128)S(1)}, f32[8,128]{1,0:T(8,128)S(1)}, u32[]{:S(2)}, u32[]{:S(2)}) collective-permute-start(f32[8,128]{1,0:T(8,128)S(1)} %max.12), channel_id=1, source_target_pairs={{0,3},{1,2},{2,1},{3,0},{4,7},{5,6},{6,5},{7,4},{8,11},{9,10},{10,... | collective-permute-start | bytes 12296 | tf_op jit(solution)/shard_map/ppermute | solution.py:407
  20.6 3.0 %collective-permute-start.4 = (f32[8,128]{1,0:T(8,128)S(1)}, f32[8,128]{1,0:T(8,128)S(1)}, u32[]{:S(2)}, u32[]{:S(2)}) collective-permute-start(f32[8,128]{1,0:T(8,128)S(1)} %max.13), channel_id=1, source_target_pairs={{0,5},{1,4},{2,7},{3,6},{4,1},{5,0},{6,3},{7,2},{8,13},{9,12},{10,... | collective-permute-start | bytes 12296 | tf_op jit(solution)/shard_map/ppermute | solution.py:407
  23.7 4.1 %collective-permute-start.5 = (f32[8,128]{1,0:T(8,128)S(1)}, f32[8,128]{1,0:T(8,128)S(1)}, u32[]{:S(2)}, u32[]{:S(2)}) collective-permute-start(f32[8,128]{1,0:T(8,128)S(1)} %max.14), channel_id=1, source_target_pairs={{0,9},{1,8},{2,11},{3,10},{4,13},{5,12},{6,15},{7,14},{8,1},{9,0},... | collective-permute-start | bytes 12296 | tf_op jit(solution)/shard_map/ppermute | solution.py:407

commit v2 on v0

--- a/solution.py
+++ b/solution.py
@@ -18,6 +18,8 @@
 LANES = 128
 GIVEN = 32
 TAKEN = 32
+SLOTS = 8
+DELAY = 4
 SPREAD = 32
 TABLE = 16
 
@@ -330,41 +332,62 @@
     half = lax.broadcasted_iota(jnp.int32, (2, LANES), 0)
 
     def visit(group, top):
-        found = []
-        for u in range(TAKEN):
-            v = group * TAKEN + u
-            block = listed_ref[3, v]
-            base = listed_ref[4, v]
-            rel = relative(cells_ref, block, listed_ref[5, v])
-            hot = one_hot(rel, WIDE)
-            rows = []
-            for a in range(2):
-                three = [pair_ref[base + a * (NY + 1) + k] for k in range(3)]
-                rows += [jnp.concatenate(three[b : b + 2], axis=1) for b in range(2)]
-            both = jnp.dot(jnp.concatenate(rows, axis=0), hot, preferred_element_type=f32)
-            corners = []
-            for k in range(4):
-                four = both[2 * TABLE * k : 2 * TABLE * (k + 1)]
-                corners += [four[0:8] + four[16:24], four[8:16] + four[24:32]]
-            here = pl.ds(pl.multiple_of(block * BLOCK, BLOCK), BLOCK)
-            frac = frac_ref[:, here]
-            for d in (2, 1, 0):
-                share = frac[d : d + 1, :]
-                corners = [
-                    corners[k] + share * (corners[k + 1] - corners[k])
-                    for k in range(0, len(corners), 2)
-                ]
-            fresh = flip_share * vel_ref[:, here] + corners[0][0:3]
-            square = jnp.sum(fresh * fresh, axis=0, keepdims=True)
-            slot = block * BLOCK + half * LANES + lane
-            taken = (rel >= 0) & (rel < WIDE) & (slot < count)
-            for h in range(2):
-                part = square[:, h * LANES : (h + 1) * LANES]
-                top = jnp.maximum(top, jnp.where(taken[h : h + 1], part, 0.0))
-            found.append((block, corners[0]))
-        for block, part in found:
-            out_ref[pl.ds(block, 1)] += part[None]
-        return top
+        best = [top]
+
+        def run(*sums):
+            found = []
+            begun = []
+
+            def take(u):
+                block, rel = begun[u]
+                both = pltpu.matmul_pop(sums[u % SLOTS])
+                corners = []
+                for k in range(4):
+                    four = both[2 * TABLE * k : 2 * TABLE * (k + 1)]
+                    corners += [four[0:8] + four[16:24], four[8:16] + four[24:32]]
+                here = pl.ds(pl.multiple_of(block * BLOCK, BLOCK), BLOCK)
+                frac = frac_ref[:, here]
+                for d in (2, 1, 0):
+                    share = frac[d : d + 1, :]
+                    corners = [
+                        corners[k] + share * (corners[k + 1] - corners[k])
+                        for k in range(0, len(corners), 2)
+                    ]
+                fresh = flip_share * vel_ref[:, here] + corners[0][0:3]
+                square = jnp.sum(fresh * fresh, axis=0, keepdims=True)
+                slot = block * BLOCK + half * LANES + lane
+                taken = (rel >= 0) & (rel < WIDE) & (slot < count)
+                for h in range(2):
+                    part = square[:, h * LANES : (h + 1) * LANES]
+                    best[0] = jnp.maximum(best[0], jnp.where(taken[h : h + 1], part, 0.0))
+                found.append((block, corners[0]))
+
+            for u in range(TAKEN):
+                v = group * TAKEN + u
+                block = listed_ref[3, v]
+                base = listed_ref[4, v]
+                rel = relative(cells_ref, block, listed_ref[5, v])
+                begun.append((block, rel))
+                rows = []
+                for a in range(2):
+                    three = [pair_ref[base + a * (NY + 1) + k] for k in range(3)]
+                    rows += [jnp.concatenate(three[b : b + 2], axis=1) for b in range(2)]
+                unit, turn = u % 2, u // 2 % 2
+                pltpu.matmul_push_rhs(one_hot(rel, WIDE), turn, unit)
+                pltpu.matmul_acc_lhs(
+                    sums[u % SLOTS], jnp.concatenate(rows, axis=0), load_staged_rhs=turn
+                )
+                if u >= DELAY:
+                    take(u - DELAY)
+            for u in range(TAKEN - DELAY, TAKEN):
+                take(u)
+            for block, part in found:
+                out_ref[pl.ds(block, 1)] += part[None]
+            return best[0]
+
+        return pl.run_scoped(
+            run, *[pltpu.ACC(k % 2)((8 * TABLE, WIDE), f32) for k in range(SLOTS)]
+        )
 
     top = jnp.zeros((1, LANES), f32)
     for group in range(2):

time: 28.3 us -> 27.8 us (0.982)
  starting transfers between devices: 7.42 us -> 10.6 us
  waiting for transfers between devices: 9.58 us -> 7.43 us
  Pallas kernels: 8.64 us -> 7.1 us
    ppermute x4, starting transfers between devices: 1.92 us -> 4.26 us  [largest(): value = jnp.maximum(value, lax.ppermute(value, axis, pairs))]
    ppermute x4, waiting for transfers between devices: 8.22 us -> 6.08 us  [largest(): value = jnp.maximum(value, lax.ppermute(value, axis, pairs))]
    pallas_call x1, Pallas kernels: 3.85 us -> 3.01 us  [body(): pl.pallas_call(spread_kernel, out_shape=(pltpu.VMEM((4 * CX, NY, NZ), f32...]
    ppermute x1, starting transfers between devices: 5.5 us -> 6.33 us  [body(): far_new = lax.ppermute(far, 'gx', far_pairs)]
    pallas_call x1, Pallas kernels: 3.72 us -> 3.01 us  [body(): pl.pallas_call(collect_kernel, out_shape=(jax.ShapeDtypeStruct((blocks, 8...]
where the time goes in v2:
time: 27.8 us; the launch traced here: 27.6 us
  starting transfers between devices  10.6 us (38%)
  waiting for transfers between devices  7.43 us (27%)
  Pallas kernels  7.1 us (26%)
  between operations  1.96 us (7%)
  local copies, waits for them, and re-layouts  0.52 us (2%)
    ppermute x1, starting transfers between devices, body(): far_new = lax.ppermute(far, 'gx', far_pairs)  6.33 us
    ppermute x4, waiting for transfers between devices, largest(): value = jnp.maximum(value, lax.ppermute(value, axis, pairs))  6.08 us
    ppermute x4, starting transfers between devices, largest(): value = jnp.maximum(value, lax.ppermute(value, axis, pairs))  4.26 us
    pallas_call x1, Pallas kernels, body(): pl.pallas_call(spread_kernel, out_shape=(pltpu.VMEM((4 * CX, NY, NZ), f32...  3.01 us
    pallas_call x1, Pallas kernels, body(): pl.pallas_call(collect_kernel, out_shape=(jax.ShapeDtypeStruct((blocks, 8...  3.01 us
    ppermute x1, waiting for transfers between devices, body(): far_new = lax.ppermute(far, 'gx', far_pairs)  1.35 us
    pallas_call x1, Pallas kernels, body(): pl.pallas_call(finish_kernel, out_shape=(jax.ShapeDtypeStruct(frac.shape,...  1.08 us
  transfers between devices with their start and end apart: 6, of which 5 were waited for; matrix products, arithmetic and copies ran while one was open for 0% of the time, Pallas kernels for 4%

profile of v2, /device:TPU:0, one launch (start us, length us, event | category | flops | bytes accessed | tf_op | source)
XLA Modules:
  0.0 27.6 jit_solution(5667179870949561340)
XLA Ops:
  0.6 3.0 %spread.1 = (f32[8,32,128]{2,1,0:T(8,128)S(1)}, f32[8,32,128]{2,1,0:T(8,128)S(1)}, f32[12,32,128]{2,1,0:T(8,128)S(1)}, s32[8,128]{1,0:T(8,128)S(1)}, f32[3,16384...) custom-call(f32[3,16384]{1,0:T(4,128)} %frac_hbm.1, f32[3,16384]{1,0:T(4,128)} %vel_hbm.1, ...), custom_call_target="tpu_custom_call" | custom-call | tf_op jit(solution)/shard_map/spread/pallas_call | solution.py:439
  3.6 6.3 %collective-permute-start = (f32[8,32,128]{2,1,0:T(8,128)S(1)}, f32[8,32,128]{2,1,0:T(8,128)S(1)}, u32[]{:S(2)}, u32[]{:S(2)}) collective-permute-start(f32[8,32,128]{2,1,0:T(8,128)S(1)} %get-tuple-element.17), channel_id=1, source_target_pairs={{0,15},{1,2},{2,1},{3,4},{4,3},{5,6},{6,5},{7,8},{8,7},{9,10},{10,... | collective-permute-start | bytes 393224 | tf_op jit(solution)/shard_map/ppermute | solution.py:465
  10.0 0.0 collective-permute-start.1
  11.3 1.4 %collective-permute-done.far_new_ref = f32[8,32,128]{2,1,0:T(8,128)S(1)} collective-permute-done((f32[8,32,128]{2,1,0:T(8,128)S(1)}, f32[8,32,128]{2,1,0:T(8,128)S(1)}, u32[]{:S(2)}, u32[]{:S(2)}) %collective-permute-start) | collective-permute-done | bytes 131104 | tf_op jit(solution)/shard_map/ppermute | solution.py:465
  12.6 0.0 collective-permute-done.1.near_new_ref
  12.6 3.0 %collect.1 = (f32[64,8,256]{2,1,0:T(8,128)S(1)}, f32[8,128]{1,0:T(8,128)S(1)}) custom-call(f32[1]{0:T(128)S(6)} %copy.10.step_ref, s32[1]{0:T(128)S(6)} %copy.9.count_ref, s32[8,128]{1,0:T(8,128)S(1)} %get-tuple-element.15.plan_ref, f32[12,32,128]{2,1,0:T(8,128)S(1)} %get-tuple-element.16.layers_ref, f32[8,32,128]{2,1,0:T(8,128)S(1)} %collective-permute-done.far_new_ref, ...), custom_call_target="tpu_custom_call" | custom-call | tf_op jit(solution)/shard_map/collect/pallas_call | solution.py:467
  15.7 0.1 collective-permute-start.2
  15.7 1.2 %collective-permute-done.2 = f32[8,128]{1,0:T(8,128)S(1)} collective-permute-done((f32[8,128]{1,0:T(8,128)S(1)}, f32[8,128]{1,0:T(8,128)S(1)}, u32[]{:S(2)}, u32[]{:S(2)}) %collective-permute-start.2) | collective-permute-done | bytes 4128 | tf_op jit(solution)/shard_map/ppermute | solution.py:424
  16.9 1.4 %collective-permute-start.3 = (f32[8,128]{1,0:T(8,128)S(1)}, f32[8,128]{1,0:T(8,128)S(1)}, u32[]{:S(2)}, u32[]{:S(2)}) collective-permute-start(f32[8,128]{1,0:T(8,128)S(1)} %max.12), channel_id=1, source_target_pairs={{0,3},{1,2},{2,1},{3,0},{4,7},{5,6},{6,5},{7,4},{8,11},{9,10},{10,... | collective-permute-start | bytes 12296 | tf_op jit(solution)/shard_map/ppermute | solution.py:424
  18.3 1.6 %collective-permute-done.3 = f32[8,128]{1,0:T(8,128)S(1)} collective-permute-done((f32[8,128]{1,0:T(8,128)S(1)}, f32[8,128]{1,0:T(8,128)S(1)}, u32[]{:S(2)}, u32[]{:S(2)}) %collective-permute-start.3) | collective-permute-done | bytes 4128 | tf_op jit(solution)/shard_map/ppermute | solution.py:424
  19.9 0.0 collective-permute-start.4
  19.9 3.0 %collective-permute-done.4 = f32[8,128]{1,0:T(8,128)S(1)} collective-permute-done((f32[8,128]{1,0:T(8,128)S(1)}, f32[8,128]{1,0:T(8,128)S(1)}, u32[]{:S(2)}, u32[]{:S(2)}) %collective-permute-start.4) | collective-permute-done | bytes 4128 | tf_op jit(solution)/shard_map/ppermute | solution.py:424
  23.0 2.8 %collective-permute-start.5 = (f32[8,128]{1,0:T(8,128)S(1)}, f32[8,128]{1,0:T(8,128)S(1)}, u32[]{:S(2)}, u32[]{:S(2)}) collective-permute-start(f32[8,128]{1,0:T(8,128)S(1)} %max.14), channel_id=1, source_target_pairs={{0,9},{1,8},{2,11},{3,10},{4,13},{5,12},{6,15},{7,14},{8,1},{9,0},... | collective-permute-start | bytes 12296 | tf_op jit(solution)/shard_map/ppermute | solution.py:424
  25.8 1.1 %finish.1 = (f32[3,16384]{1,0:T(4,128)}, f32[3,16384]{1,0:T(4,128)}) custom-call(s32[128,128]{1,0:T(8,128)S(1)} %get-tuple-element.14.cells_ref, f32[64,8,256]{2,1,0:T(8,128)S(1)} %get-tuple-element.21.moved_ref, f32[3,16384]{1,0:T(4,128)S(1)} %get-tuple-element.19.frac_ref, f32[3,16384]{1,0:T(4,128)S(1)} %get-tuple-element.20.vel_ref), custom_call_target="tpu_custom_call" | custom-call | bytes 8000000 | tf_op jit(solution)/shard_map/finish/pallas_call | solution.py:484
  26.8 0.3 collective-permute-done.5
  27.1 0.5 %slice.3 = f32[1,1]{1,0:T(1,128)} slice(f32[8,128]{1,0:T(8,128)S(1)} %add_divide_fusion), slice={[0:1], [0:1]} | slice | bytes 8 | tf_op jit(solution)/shard_map/slice | solution.py:497
  (4 shorter events, 0.0 us)
Async XLA Ops:
  3.6 9.0 %collective-permute-start = (f32[8,32,128]{2,1,0:T(8,128)S(1)}, f32[8,32,128]{2,1,0:T(8,128)S(1)}, u32[]{:S(2)}, u32[]{:S(2)}) collective-permute-start(f32[8,32,128]{2,1,0:T(8,128)S(1)} %get-tuple-element.17), channel_id=1, source_target_pairs={{0,15},{1,2},{2,1},{3,4},{4,3},{5,6},{6,5},{7,8},{8,7},{9,10},{10,... | collective-permute-start | bytes 393224 | tf_op jit(solution)/shard_map/ppermute | solution.py:465
  10.0 2.7 %collective-permute-start.1 = (f32[8,32,128]{2,1,0:T(8,128)S(1)}, f32[8,32,128]{2,1,0:T(8,128)S(1)}, u32[]{:S(2)}, u32[]{:S(2)}) collective-permute-start(f32[8,32,128]{2,1,0:T(8,128)S(1)} %get-tuple-element.18), channel_id=1, source_target_pairs={{0,1},{1,0},{2,3},{3,2},{4,5},{5,4},{6,7},{7,6},{8,9},{9,8},{10,11... | collective-permute-start | bytes 393224 | tf_op jit(solution)/shard_map/ppermute | solution.py:466
  15.7 1.2 %collective-permute-start.2 = (f32[8,128]{1,0:T(8,128)S(1)}, f32[8,128]{1,0:T(8,128)S(1)}, u32[]{:S(2)}, u32[]{:S(2)}) collective-permute-start(f32[8,128]{1,0:T(8,128)S(1)} %get-tuple-element.24), channel_id=1, source_target_pairs={{0,1},{1,0},{2,3},{3,2},{4,5},{5,4},{6,7},{7,6},{8,9},{9,8},{10,11... | collective-permute-start | bytes 12296 | tf_op jit(solution)/shard_map/ppermute | solution.py:424
  16.9 3.0 %collective-permute-start.3 = (f32[8,128]{1,0:T(8,128)S(1)}, f32[8,128]{1,0:T(8,128)S(1)}, u32[]{:S(2)}, u32[]{:S(2)}) collective-permute-start(f32[8,128]{1,0:T(8,128)S(1)} %max.12), channel_id=1, source_target_pairs={{0,3},{1,2},{2,1},{3,0},{4,7},{5,6},{6,5},{7,4},{8,11},{9,10},{10,... | collective-permute-start | bytes 12296 | tf_op jit(solution)/shard_map/ppermute | solution.py:424
  19.9 3.0 %collective-permute-start.4 = (f32[8,128]{1,0:T(8,128)S(1)}, f32[8,128]{1,0:T(8,128)S(1)}, u32[]{:S(2)}, u32[]{:S(2)}) collective-permute-start(f32[8,128]{1,0:T(8,128)S(1)} %max.13), channel_id=1, source_target_pairs={{0,5},{1,4},{2,7},{3,6},{4,1},{5,0},{6,3},{7,2},{8,13},{9,12},{10,... | collective-permute-start | bytes 12296 | tf_op jit(solution)/shard_map/ppermute | solution.py:424
  23.0 4.1 %collective-permute-start.5 = (f32[8,128]{1,0:T(8,128)S(1)}, f32[8,128]{1,0:T(8,128)S(1)}, u32[]{:S(2)}, u32[]{:S(2)}) collective-permute-start(f32[8,128]{1,0:T(8,128)S(1)} %max.14), channel_id=1, source_target_pairs={{0,9},{1,8},{2,11},{3,10},{4,13},{5,12},{6,15},{7,14},{8,1},{9,0},... | collective-permute-start | bytes 12296 | tf_op jit(solution)/shard_map/ppermute | solution.py:424
